TPU v7x, 128 devices: a whole 4x4x4 slice. The times are simulated.
128 devices in a mesh: row: 4 (over x), col: 2 (over core), depth: 16 (over z, y).
Axes of the slice: x: 4, y: 4, z: 4, core: 2. Of those that a mesh axis runs over, the one named last changes fastest.
Arguments:
- grad_out: bfloat16 [16, 512, 4096], P('depth', 'row', 'col'), may hold values from -6 to 6
- gate_pre: bfloat16 [16, 512, 14336], P('depth', 'col', 'row'), may hold values from -8 to 8
- up_pre: bfloat16 [16, 512, 14336], P('depth', 'col', 'row'), may hold values from -6 to 6
- down_weight: bfloat16 [14336, 4096], P('row', 'col'), may hold values from -0.09375 to 0.09375
Outputs:
- grad_gate: bfloat16 [16, 512, 14336], P('depth', 'col', 'row')
- grad_up: bfloat16 [16, 512, 14336], P('depth', 'col', 'row')
- grad_weight: bfloat16 [14336, 4096], P('row', ('col', 'depth'))
All inputs are finite; a program needn't handle non-finite values.
Results may differ from a plain program's by a relative error of at most 0.019.
Values may be sent and summed in bfloat16 or wider, within the bound.
A program may use at most 128 MiB of HBM per device.

v0:
```python
import jax
import jax.numpy as jnp
from jax import lax
from jax.sharding import PartitionSpec as P


def on_device(grad_out, gate_pre, up_pre, down_weight):
    gate_value = gate_pre[0].astype(jnp.float32)
    up_value = up_pre[0].astype(jnp.float32)
    sigmoid_gate = jax.nn.sigmoid(gate_value)
    silu_gate = gate_value * sigmoid_gate
    hidden = (silu_gate * up_value).astype(jnp.bfloat16)
    local_tokens = hidden.shape[0]
    panel_rows = lax.all_gather(grad_out, "row", axis=1, tiled=True)[0]
    partial_sum = lax.dot_general(
        panel_rows, down_weight, (((1,), (1,)), ((), ())), preferred_element_type=jnp.float32
    )
    summed = lax.psum(partial_sum.astype(jnp.bfloat16), "col").astype(jnp.float32)
    offset = lax.axis_index("col") * local_tokens
    grad_hidden = lax.dynamic_slice_in_dim(summed, offset, local_tokens, 0)
    derivative = sigmoid_gate * (1.0 + gate_value * (1.0 - sigmoid_gate))
    grad_gate = (grad_hidden * up_value * derivative).astype(jnp.bfloat16)
    grad_up = (grad_hidden * silu_gate).astype(jnp.bfloat16)
    weight_partial = lax.dot_general(
        lax.all_gather(hidden[None], "col", axis=1, tiled=True)[0],
        panel_rows,
        (((0,), (0,)), ((), ())),
        preferred_element_type=jnp.float32,
    )
    weight_total = lax.psum_scatter(
        weight_partial.astype(jnp.bfloat16), "depth", scatter_dimension=1, tiled=True
    ).astype(jnp.float32)
    token_scale = float(lax.axis_size("depth") * panel_rows.shape[0]) ** (-0.5)
    grad_weight = (weight_total * token_scale).astype(jnp.bfloat16)
    return (grad_gate[None], grad_up[None], grad_weight)


def solution(mesh):
    in_specs = (
        P("depth", "row", "col"),
        P("depth", "col", "row"),
        P("depth", "col", "row"),
        P("row", "col"),
    )
    out_specs = (P("depth", "col", "row"), P("depth", "col", "row"), P("row", ("col", "depth")))
    return jax.shard_map(
        on_device, mesh=mesh, in_specs=in_specs, out_specs=out_specs, check_vma=False
    )
```

profile of v0, /device:TPU:1, one launch (start us, length us, event | category | flops | bytes accessed | tf_op | source)
XLA Modules:
  0.0 211.4 jit_solution(17240666277021589257)
XLA Ops:
  7.2 0.0 all-gather.3.cloned.1.call-start
  7.2 0.7 all-gather.3.cloned.1.call-update
  7.9 0.0 all-gather.5.cloned.1.call-start
  7.9 4.4 %fusion.6 = bf16[1,256,3584]{2,1,0:T(8,128)(2,1)} fusion(bf16[1,256,3584]{2,1,0:T(8,128)(2,1)} %param.6, bf16[1,256,3584]{2,1,0:T(8,128)(2,1)} %param.5), kind=kLoop, calls=%fused_computation.15 | loop fusion | flops 7340032 | bytes 5505024 | tf_op jit(solution)/shard_map/convert_element_type | solution.py:12
  12.3 0.0 all-gather.5.cloned.1.call-update
  12.3 0.0 all-reduce.2.cloned.1.call-start
  12.4 31.3 %all-gather.3.cloned.1.call-done = bf16[1,512,2048]{2,1,0:T(8,128)(2,1)} async-done(((bf16[1,128,2048]{2,1,0:T(8,128)(2,1)}), bf16[1,512,2048]{2,1,0:T(8,128)(2,1)}) %all-gather.3.cloned.1.call-update) | async-done | bytes 2097168 | tf_op jit(solution)/shard_map/all_gather | solution.py:14
  43.7 13.0 %convolution_convert_fusion.1 = bf16[512,3584]{1,0:T(8,128)(2,1)} fusion(bf16[3584,2048]{1,0:T(8,128)(2,1)} %param.7, bf16[1,512,2048]{2,1,0:T(8,128)(2,1)} %all-gather.3.cloned.1.call-done), kind=kOutput, calls=%fused_computation.1 | convolution fusion | flops 7518027776 | bytes 20447232 | tf_op jit(solution)/shard_map/dot_general | solution.py:15
  56.7 0.0 copy-start.1
  56.7 0.0 all-reduce.2.cloned.1.call-update
  56.7 0.0 reduce-scatter.4.cloned.1.call-start
  56.8 5.3 %all-gather.5.cloned.1.call-done = bf16[1,512,3584]{2,1,0:T(8,128)(2,1)} async-done(((bf16[1,256,3584]{2,1,0:T(8,128)(2,1)}), bf16[1,512,3584]{2,1,0:T(8,128)(2,1)}) %all-gather.5.cloned.1.call-update) | async-done | bytes 3670032 | tf_op jit(solution)/shard_map/all_gather | solution.py:25
  62.0 0.0 copy-done.1
  62.0 13.7 %convolution_convert_fusion = bf16[3584,2048]{1,0:T(8,128)(2,1)} fusion(bf16[1,512,3584]{2,1,0:T(8,128)(2,1)} %all-gather.5.cloned.1.call-done, bf16[1,512,2048]{2,1,0:T(8,128)(2,1)S(1)} %copy-done.1), kind=kOutput, calls=%fused_computation | convolution fusion | flops 7523532800 | bytes 20447232 | tf_op jit(solution)/shard_map/dot_general | solution.py:24
  75.8 19.2 %copy.7 = bf16[3584,2048]{0,1:T(8,128)(2,1)} copy(bf16[3584,2048]{1,0:T(8,128)(2,1)} %convolution_convert_fusion) | data formatting | bytes 29360128
  95.0 0.0 copy-start
  95.0 0.0 reduce-scatter.4.cloned.1.call-update
  95.0 0.7 all-reduce.2.cloned.1.call-done
  95.7 0.8 copy-done
  96.5 4.7 %fusion.18 = (bf16[1,256,3584]{2,1,0:T(8,128)(2,1)}, bf16[1,256,3584]{2,1,0:T(8,128)(2,1)}) fusion(bf16[1,256,3584]{2,1,0:T(8,128)(2,1)S(1)} %copy-done, bf16[512,3584]{1,0:T(8,128)(2,1)} %all-reduce.2.cloned.1.call-done, s32[]{:T(128)S(6)} %select_n.3, bf16[1,256,3584]{2,1,0:T(8,128)(2,1)} %param.6), kind=kLoop, calls=%fused_computation.28 | loop fusion | flops 14680064 | bytes 9175044 | tf_op jit(solution)/shard_map/broadcast_in_dim | solution.py:35
  101.1 101.1 %reduce-scatter.4.cloned.1.call-done = bf16[128,3584]{1,0:T(8,128)(2,1)} async-done(((bf16[2048,3584]{1,0:T(8,128)(2,1)}), bf16[128,3584]{1,0:T(8,128)(2,1)}) %reduce-scatter.4.cloned.1.call-update) | async-done | bytes 917520
  202.2 1.5 copy.8
  203.7 1.1 multiply_convert_fusion
Async XLA Ops:
  7.2 36.5 %all-gather.3.cloned.1.call-start = ((), (), s32[]{:S(2)}) async-start(), calls=%async_computation.1 | async-start | bytes 2621440 | tf_op jit(solution)/shard_map/all_gather | solution.py:14
  7.9 54.1 %all-gather.5.cloned.1.call-start = ((), (), s32[]{:S(2)}) async-start(), calls=%async_computation.3 | async-start | bytes 5505024 | tf_op jit(solution)/shard_map/all_gather | solution.py:25
  12.3 83.3 %all-reduce.2.cloned.1.call-start = ((), (), s32[]{:S(2)}) async-start(), calls=%async_computation.2 | async-start | bytes 7340032 | tf_op jit(solution)/shard_map/psum | solution.py:18
  56.7 5.4 %copy-start.1 = (bf16[1,512,2048]{2,1,0:T(8,128)(2,1)S(1)}, bf16[1,512,2048]{2,1,0:T(8,128)(2,1)}, u32[]{:S(2)}) copy-start(bf16[1,512,2048]{2,1,0:T(8,128)(2,1)} %all-gather.3.cloned.1.call-done) | copy-start | bytes 6291460
  56.7 145.5 %reduce-scatter.4.cloned.1.call-start = ((), (), s32[]{:S(2)}) async-start(), calls=%async_computation.4 | async-start | bytes 15597568
  95.0 1.5 copy-start
Sparse Core Ops, SparseCore 0:
  9.7 34.0 all-gather.2
  45.9 16.0 all-gather.4
  64.5 31.1 all-reduce.1
  99.3 102.7 reduce-scatter.3
where the time goes:
time: 212 us; the launch traced here: 211 us
  waiting for transfers between devices  139 us (66%)
  matrix products  26.7 us (13%)
  local copies, waits for them, and re-layouts  21.5 us (10%)
  between operations  13.8 us (7%)
  other arithmetic  10.1 us (5%)
    unnamed x5, waiting for transfers between devices  102 us
    all_gather x1, waiting for transfers between devices, on_device(): panel_rows = lax.all_gather(grad_out, 'row', axis=1, tiled=True)[0]  31.3 us
    unnamed x6, local copies, waits for them, and re-layouts  21.5 us
    dot_general x1, matrix products, on_device(): lax.dot_general(lax.all_gather(hidden[None], 'col', axis=1, tiled=True)[0...  13.7 us
    dot_general x1, matrix products, on_device(): lax.dot_general(panel_rows, down_weight, (((1,), (1,)), ((), ())), prefer...  13 us
    all_gather x1, waiting for transfers between devices, on_device(): lax.all_gather(hidden[None], 'col', axis=1, tiled=True)[0]  5.28 us
    broadcast_in_dim x1, other arithmetic, on_device(): return (grad_gate[None], grad_up[None], grad_weight)  4.66 us
    convert_element_type x1, other arithmetic, on_device(): hidden = (silu_gate * up_value).astype(jnp.bfloat16)  4.38 us
  transfers between devices with their start and end apart: 4, of which 4 were waited for; matrix products, arithmetic and copies ran while one was open for 26% of the time, Pallas kernels for 0%

commit v1 on v0

v1 whole, which is shorter than its diff:
```python
import jax
import jax.numpy as jnp
from jax import lax
from jax.experimental import pallas as pl
from jax.experimental.pallas import tpu as pltpu
from jax.sharding import PartitionSpec as P

MESH = pl.DeviceIdType.MESH
BF16, F32 = jnp.bfloat16, jnp.float32

TOK, FF, DM = 512, 3584, 2048
HALF = TOK // 2
ROWS = TOK // 4
FC = 512
HF = FC // 2
NC = FF // FC
BLK = 128
STEP = 32
SCALE = float(16 * TOK) ** -0.5


def kernel(
    go, gate, up, w, o_gate, o_up, o_w,
    g_own, g_pair, g_t, hid, gate_v, up_v, wbuf, ghs, ghr, wout,
    zs0, zr0, zs1, zr1, es, er, zkeep,
    as_, ar, ys0, yr0, ys1, yr1, ykeep,
    xo_s, xo_r, xf_s, xf_r, pp_s, pp_r, px_s, px_r, pf_s, pf_r,
    hc_s, hc_r, hp_s, hp_r, hf_s, hf_r,
    z0_s, z0_r, z1_s, z1_r, e_s, e_r, a_s, a_r, y0_s, y0_r, y1_s, y1_r,
    gh_s, gh_r, ld_g, ld_u, ld_o, ld_w, st_g, st_u, st_w,
):
    x, c, q = lax.axis_index("row"), lax.axis_index("col"), lax.axis_index("depth")
    z, y = lax.div(q, 4), lax.rem(q, 4)
    odd = lax.rem(y, 2)
    y_pair = y + 1 - 2 * odd
    y_sum = lax.rem(y + 3 + 2 * odd, 4)
    y_pair_sum = lax.rem(y_pair + 3 + 2 * (1 - odd), 4)
    core = (x, 1 - c, q)
    right, left = (lax.rem(x + 1, 4), c, q), (lax.rem(x + 3, 4), c, q)
    sides = (right, left)
    pair = (x, c, z * 4 + y_pair)
    across = (x, c, z * 4 + y_sum)
    above, below = (x, c, lax.rem(z + 1, 4) * 4 + y), (x, c, lax.rem(z + 3, 4) * 4 + y)

    barrier = pltpu.get_barrier_semaphore()
    for other in (core, right, left, pair, across, above, below):
        pl.semaphore_signal(barrier, inc=1, device_id=other, device_id_type=MESH)
    pl.semaphore_wait(barrier, 7)

    def send(src, dst, ss, rs, device):
        return pltpu.make_async_remote_copy(
            src_ref=src, dst_ref=dst, send_sem=ss, recv_sem=rs, device_id=device, device_id_type=MESH
        )

    def ds(start, size, unit):
        return pl.ds(pl.multiple_of(start, unit), size)

    def layer(j):
        return lax.rem(z + jnp.where(j == 0, 2, jnp.where(j == 1, 1, jnp.where(j == 2, 3, 0))), 4)

    def block_of(j, s):
        column = (y, y_sum, y_pair, y_pair_sum)[s]
        return layer(j) * 4 + column

    def cols(b):
        return ds(b * BLK, BLK, BLK)

    def own_copy():
        return pltpu.make_async_copy(go, g_own.at[ds(x * ROWS, ROWS, ROWS)], ld_o)

    def own_direct(b, side):
        return send(
            go.at[:, cols(b)], g_own.at[ds(x * ROWS, ROWS, ROWS), cols(b)],
            xo_s.at[b, side], xo_r.at[b, side], sides[side],
        )

    def own_forward(b, side):
        source = lax.rem(x + (3 if side == 0 else 1), 4)
        rows = ds(source * ROWS + side * (ROWS // 2), ROWS // 2, ROWS // 2)
        return send(
            g_own.at[rows, cols(b)], g_own.at[rows, cols(b)], xf_s.at[b, side], xf_r.at[b, side], sides[side]
        )

    def pair_send(j, s):
        i = j * 2 + s
        return send(
            go.at[:, cols(block_of(j, s + 2))], g_pair.at[ds(x * ROWS, ROWS, ROWS), cols(i)],
            pp_s.at[i], pp_r.at[i], pair,
        )

    def pair_cols(j):
        return ds(j * 2 * BLK, 2 * BLK, 2 * BLK)

    def pair_direct(j, side):
        view = g_pair.at[ds(x * ROWS, ROWS, ROWS), pair_cols(j)]
        return send(view, view, px_s.at[j, side], px_r.at[j, side], sides[side])

    def pair_forward(j, side):
        source = lax.rem(x + (3 if side == 0 else 1), 4)
        view = g_pair.at[ds(source * ROWS + side * (ROWS // 2), ROWS // 2, ROWS // 2), pair_cols(j)]
        return send(view, view, pf_s.at[j, side], pf_r.at[j, side], sides[side])

    def own_start(j, first):
        for s in (first, first + 1):
            for side in (0, 1):
                own_direct(block_of(j, s), side).start()

    def own_pass(j, first):
        for s in (first, first + 1):
            b = block_of(j, s)
            for side in (0, 1):
                own_direct(b, side).wait_recv()
                own_forward(b, side).start()

    def own_end(j, first):
        for s in (first, first + 1):
            for side in (0, 1):
                own_forward(block_of(j, s), side).wait_recv()

    def in_copy(k, src, dst, sem):
        f = ds(k * FC, FC, FC)
        return pltpu.make_async_copy(src.at[:, f], dst.at[:, f], sem.at[k])

    def hid_view(group, half, k):
        return hid.at[ds(group * TOK + half * HALF, HALF, HALF), ds(k * FC, FC, FC)]

    def hid_core(k):
        return send(hid_view(0, c, k), hid_view(0, c, k), hc_s.at[k], hc_r.at[k], core)

    def hid_pair(k):
        return send(hid_view(0, c, k), hid_view(1, c, k), hp_s.at[k], hp_r.at[k], pair)

    def hid_pass(k):
        return send(hid_view(1, c, k), hid_view(1, c, k), hf_s.at[k], hf_r.at[k], core)

    def make_hidden(k):
        in_copy(k, gate, gate_v, ld_g).wait()
        in_copy(k, up, up_v, ld_u).wait()
        f = ds(k * FC, FC, FC)

        def rows(i, carry):
            r = ds(i * STEP, STEP, STEP)
            g = gate_v[r, f].astype(F32)
            u = up_v[r, f].astype(F32)
            hid[ds(c * HALF + i * STEP, STEP, STEP), f] = (g * (1.0 / (1.0 + jnp.exp(-g))) * u).astype(BF16)
            return carry

        lax.fori_loop(0, HALF // STEP, rows, 0)
        hid_pair(k).start()
        hid_core(k).start()

    def dot(rows, k, part):
        return jnp.dot(rows, hid[:, ds(k * FC + part * HF, HF, HF)], preferred_element_type=F32)

    def of_layer(j):
        return g_t[2 * BLK * j : 2 * BLK * (j + 1), :]

    def of_column(s, h):
        return jnp.concatenate(
            [g_t[(4 * h + s) * BLK : (4 * h + s + 1) * BLK, :], g_t[(4 * h + 2 + s) * BLK : (4 * h + 3 + s) * BLK, :]], 0
        )

    def z0(k, half):
        return send(zs0.at[k, half], zr0.at[k, half], z0_s.at[k, half], z0_r.at[k, half], (below, above)[half])

    def z1(k, way):
        return send(zs1.at[k, way], zr1.at[k, way], z1_s.at[k, way], z1_r.at[k, way], (above, below)[way])

    def z_last(k):
        return send(es.at[k], er.at[k], e_s.at[k], e_r.at[k], across)

    def y_first(k):
        return send(as_.at[k], ar.at[k], a_s.at[k], a_r.at[k], across)

    def y0(k, half):
        return send(ys0.at[k, half], yr0.at[k, half], y0_s.at[k, half], y0_r.at[k, half], (below, above)[half])

    def y1(k, way):
        return send(ys1.at[k, way], yr1.at[k, way], y1_s.at[k, way], y1_r.at[k, way], (above, below)[way])

    def stage0(k):
        part = dot(of_layer(0), k, 1).astype(BF16)
        for half in (0, 1):
            zs0[k, half] = part[:, half * BLK : (half + 1) * BLK]
            z0(k, half).start()
        for h in (0, 1):
            as_[k, 2 * BLK * h : 2 * BLK * (h + 1), :] = dot(of_column(1, h), k, 0).astype(BF16)
        y_first(k).start()

    def stage1(k):
        for way in (0, 1):
            part = dot(of_layer(1 + way), k, 1)
            half = 1 - way
            z0(k, half).wait_recv()
            lo, hi = part[:, :BLK], part[:, BLK:]
            got = zr0[k, half].astype(F32)
            if half:
                hi = hi + got
            else:
                lo = lo + got
            zs1[k, way, :, :BLK] = lo.astype(BF16)
            zs1[k, way, :, BLK:] = hi.astype(BF16)
            z1(k, way).start()
        parts = [dot(of_column(0, h), k, 0) for h in (0, 1)]
        y_first(k).wait_recv()
        first = parts[0] + ar[k, : 2 * BLK, :].astype(F32)
        far = first[:BLK, :].astype(BF16)
        for half in (0, 1):
            ys0[k, half] = far[:, half * BLK : (half + 1) * BLK]
            y0(k, half).start()
        ykeep[k, :BLK, :] = first[BLK:, :]
        ykeep[k, BLK:, :] = parts[1] + ar[k, 2 * BLK :, :].astype(F32)

    def stage2(k):
        for way in (0, 1):
            half = 1 - way
            y0(k, half).wait_recv()
            got = yr0[k, half].astype(F32)
            lo, hi = ykeep[k, BLK * way : BLK * (way + 1), :BLK], ykeep[k, BLK * way : BLK * (way + 1), BLK:]
            if half:
                hi = hi + got
            else:
                lo = lo + got
            ys1[k, way, :, :BLK] = lo.astype(BF16)
            ys1[k, way, :, BLK:] = hi.astype(BF16)
            y1(k, way).start()
        part = dot(of_layer(3), k, 1)
        for way in (0, 1):
            z1(k, way).wait_recv()
            part = part + zr1[k, way].astype(F32)
        es[k] = part[BLK:, :].astype(BF16)
        z_last(k).start()
        zkeep[k] = part[:BLK, :]

    def out_copy(k):
        f = ds(k * FC, FC, FC)
        return pltpu.make_async_copy(wout.at[f], o_w.at[f], st_w.at[k])

    def stage3(k):
        total = ykeep[k, 2 * BLK :, :]
        for way in (0, 1):
            y1(k, way).wait_recv()
            total = total + yr1[k, way].astype(F32)
        wout[ds(k * FC, HF, HF), :] = (total * SCALE).T.astype(BF16)
        z_last(k).wait_recv()
        total = zkeep[k] + er[k].astype(F32)
        wout[ds(k * FC + HF, HF, HF), :] = (total * SCALE).T.astype(BF16)
        out_copy(k).start()

    def w_copy(k):
        slot = lax.rem(k, 2)
        return pltpu.make_async_copy(w.at[ds(k * FC, FC, FC)], wbuf.at[slot], ld_w.at[slot])

    def gh_send(k):
        return send(ghs.at[k, ds((1 - c) * HALF, HALF, HALF)], ghr.at[k], gh_s.at[k], gh_r.at[k], core)

    def grad_hidden(k):
        w_copy(k).wait()

        def tile(n, carry):
            f = ds(n * HF, HF, HF)
            ghs[k, :, f] = lax.dot_general(
                g_own[...], wbuf[lax.rem(k, 2), f, :], (((1,), (1,)), ((), ())), preferred_element_type=F32
            ).astype(BF16)
            return carry

        lax.fori_loop(0, 2, tile, 0)
        gh_send(k).start()

        @pl.when(k + 2 < NC)
        def _():
            w_copy(k + 2).start()

    def gate_out(k):
        f = ds(k * FC, FC, FC)
        return (
            pltpu.make_async_copy(gate_v.at[:, f], o_gate.at[:, f], st_g.at[k]),
            pltpu.make_async_copy(up_v.at[:, f], o_up.at[:, f], st_u.at[k]),
        )

    def grad_gate(k):
        gh_send(k).wait_recv()
        f = ds(k * FC, FC, FC)

        def rows(i, carry):
            r = ds(i * STEP, STEP, STEP)
            g = gate_v[r, f].astype(F32)
            u = up_v[r, f].astype(F32)
            grad = ghs[k, ds(c * HALF + i * STEP, STEP, STEP), :].astype(F32) + ghr[k, r, :].astype(F32)
            sig = 1.0 / (1.0 + jnp.exp(-g))
            gate_v[r, f] = (grad * u * (sig * (1.0 + g * (1.0 - sig)))).astype(BF16)
            up_v[r, f] = (grad * (g * sig)).astype(BF16)
            return carry

        lax.fori_loop(0, HALF // STEP, rows, 0)
        for copy in gate_out(k):
            copy.start()

    def loads(k, carry):
        in_copy(k, gate, gate_v, ld_g).start()
        in_copy(k, up, up_v, ld_u).start()
        return carry

    own_start(0, 0)
    for s in (0, 1):
        pair_send(0, s).start()
    lax.fori_loop(0, NC, loads, 0)
    own_copy().start()
    w_copy(0).start()
    w_copy(1).start()

    def first_hidden(k, carry):
        make_hidden(k)

        @pl.when(k == 0)
        def _():
            for j in (1, 2, 3):
                for s in (0, 1):
                    pair_send(j, s).start()

        return carry

    lax.fori_loop(0, 2, first_hidden, 0)
    own_copy().wait()

    def gather(j, carry):
        @pl.when(j < 3)
        def _():
            own_start(j + 1, 0)

        for s in (0, 1):
            pair_send(j, s).wait_recv()
        for side in (0, 1):
            pair_direct(j, side).start()
        own_pass(j, 0)
        for side in (0, 1):
            pair_direct(j, side).wait_recv()
            pair_forward(j, side).start()

        @pl.when(j == 3)
        def _():
            def rest(i, carry):
                own_start(i, 2)
                return carry

            lax.fori_loop(0, 4, rest, 0)

        own_end(j, 0)
        for side in (0, 1):
            pair_forward(j, side).wait_recv()
        for s in (0, 1):
            rows = ds((j * 2 + s) * BLK, BLK, BLK)
            g_t[rows, :TOK] = g_own[:, cols(block_of(j, s))].T
            g_t[rows, TOK:] = g_pair[:, cols(j * 2 + s)].T
        return carry

    lax.fori_loop(0, 4, gather, 0)
    hid_pair(0).wait_recv()
    hid_pass(0).start()

    def body(i, carry):
        @pl.when(i + 2 < NC)
        def _():
            make_hidden(i + 2)

        @pl.when(i < NC)
        def _():
            hid_core(i).wait_recv()
            hid_pass(i).wait_recv()
            stage0(i)

        @pl.when(jnp.logical_and(i >= 1, i < NC + 1))
        def _():
            stage1(i - 1)

        @pl.when(jnp.logical_and(i >= 2, i < NC + 2))
        def _():
            stage2(i - 2)

        @pl.when(jnp.logical_and(i >= 3, i < NC + 3))
        def _():
            stage3(i - 3)

        @pl.when(i < 4)
        def _():
            own_pass(i, 2)

        @pl.when(i == 3)
        def _():
            def rest(j, carry):
                own_end(j, 2)
                return carry

            lax.fori_loop(0, 4, rest, 0)

        @pl.when(jnp.logical_and(i >= 3, i < NC + 3))
        def _():
            grad_hidden(i - 3)

        @pl.when(i >= 4)
        def _():
            grad_gate(i - 4)

        @pl.when(i + 1 < NC)
        def _():
            hid_pair(i + 1).wait_recv()
            hid_pass(i + 1).start()

        return carry

    lax.fori_loop(0, NC + 4, body, 0)

    def sent(k, carry):
        hid_core(k).wait_send()
        hid_pair(k).wait_send()
        hid_pass(k).wait_send()
        for i in (0, 1):
            z0(k, i).wait_send()
            z1(k, i).wait_send()
            y0(k, i).wait_send()
            y1(k, i).wait_send()
        z_last(k).wait_send()
        y_first(k).wait_send()
        gh_send(k).wait_send()
        for copy in gate_out(k):
            copy.wait()
        out_copy(k).wait()
        return carry

    lax.fori_loop(0, NC, sent, 0)

    def sent_x(j, carry):
        for s in range(4):
            for side in (0, 1):
                own_direct(block_of(j, s), side).wait_send()
                own_forward(block_of(j, s), side).wait_send()
        for s in (0, 1):
            pair_send(j, s).wait_send()
        for side in (0, 1):
            pair_direct(j, side).wait_send()
            pair_forward(j, side).wait_send()
        return carry

    lax.fori_loop(0, 4, sent_x, 0)


def on_device(grad_out, gate_pre, up_pre, down_weight):
    dma = pltpu.SemaphoreType.DMA
    vmem = lambda *shape: pltpu.VMEM(shape, BF16)
    scratch = [
        vmem(TOK, DM), vmem(TOK, 8 * BLK), vmem(8 * BLK, 2 * TOK), vmem(2 * TOK, FF),
        vmem(HALF, FF), vmem(HALF, FF), vmem(2, FC, DM), vmem(NC, TOK, FC), vmem(NC, HALF, FC), vmem(FF, BLK),
        vmem(NC, 2, 2 * BLK, BLK), vmem(NC, 2, 2 * BLK, BLK), vmem(NC, 2, 2 * BLK, HF), vmem(NC, 2, 2 * BLK, HF),
        vmem(NC, BLK, HF), vmem(NC, BLK, HF), pltpu.VMEM((NC, BLK, HF), F32),
        vmem(NC, 4 * BLK, HF), vmem(NC, 4 * BLK, HF), vmem(NC, 2, BLK, BLK), vmem(NC, 2, BLK, BLK),
        vmem(NC, 2, BLK, HF), vmem(NC, 2, BLK, HF), pltpu.VMEM((NC, 3 * BLK, HF), F32),
        dma((16, 2)), dma((16, 2)), dma((16, 2)), dma((16, 2)), dma((8,)), dma((8,)),
        dma((4, 2)), dma((4, 2)), dma((4, 2)), dma((4, 2)),
        dma((NC,)), dma((NC,)), dma((NC,)), dma((NC,)), dma((NC,)), dma((NC,)),
        dma((NC, 2)), dma((NC, 2)), dma((NC, 2)), dma((NC, 2)), dma((NC,)), dma((NC,)),
        dma((NC,)), dma((NC,)), dma((NC, 2)), dma((NC, 2)), dma((NC, 2)), dma((NC, 2)),
        dma((NC,)), dma((NC,)), dma((NC,)), dma((NC,)), dma, dma((2,)), dma((NC,)), dma((NC,)), dma((NC,)),
    ]
    anywhere = pl.BlockSpec(memory_space=pl.ANY)
    grad_gate, grad_up, grad_weight = pl.pallas_call(
        kernel,
        out_shape=(
            jax.ShapeDtypeStruct((HALF, FF), BF16),
            jax.ShapeDtypeStruct((HALF, FF), BF16),
            jax.ShapeDtypeStruct((FF, BLK), BF16),
        ),
        in_specs=[anywhere] * 4,
        out_specs=(anywhere,) * 3,
        scratch_shapes=scratch,
        compiler_params=pltpu.CompilerParams(
            collective_id=0, has_side_effects=True, vmem_limit_bytes=60 * 2**20
        ),
        cost_estimate=pl.CostEstimate(flops=4 * TOK * FF * DM, bytes_accessed=24 * 10**6, transcendentals=2 * HALF * FF),
    )(grad_out[0], gate_pre[0], up_pre[0], down_weight)
    return grad_gate[None], grad_up[None], grad_weight


def solution(mesh):
    in_specs = (
        P("depth", "row", "col"),
        P("depth", "col", "row"),
        P("depth", "col", "row"),
        P("row", "col"),
    )
    out_specs = (P("depth", "col", "row"), P("depth", "col", "row"), P("row", ("col", "depth")))
    return jax.shard_map(
        on_device, mesh=mesh, in_specs=in_specs, out_specs=out_specs, check_vma=False
    )
```

time: 212 us -> 119 us (0.56)
  waiting for transfers between devices: 139 us -> 0 us
  Pallas kernels: 0 us -> 113 us
  matrix products: 26.7 us -> 0 us
  local copies, waits for them, and re-layouts: 21.5 us -> 5.72 us
  between operations: 13.8 us -> 0.65 us
  other arithmetic: 10.1 us -> 0 us
    pallas_call x0 -> x1, Pallas kernels: none -> 113 us  [on_device(): pl.pallas_call(kernel, out_shape=(jax.ShapeDtypeStruct((HALF, FF), BF16),...]
    unnamed x5 -> x0, waiting for transfers between devices: 102 us -> none
    all_gather x2 -> x0, waiting for transfers between devices: 36.6 us -> none  [the longest x1 31.3 us: on_device(): panel_rows = lax.all_gather(grad_out, 'row', axis=1, tiled=True)[0]]
    dot_general x2 -> x0, matrix products: 26.7 us -> none  [the longest x1 13.7 us: on_device(): lax.dot_general(lax.all_gather(hidden[None], 'col', axis=1, tiled=True)[0...]
    unnamed x6 -> x7, local copies, waits for them, and re-layouts: 21.5 us -> 5.72 us
    convert_element_type x2 -> x0, other arithmetic: 5.48 us -> none  [the longest x1 4.38 us: on_device(): hidden = (silu_gate * up_value).astype(jnp.bfloat16)]
    broadcast_in_dim x1 -> x0, other arithmetic: 4.66 us -> none  [on_device(): return (grad_gate[None], grad_up[None], grad_weight)]
  transfers between devices with their start and end apart: 4 -> 0, of which waited for: 4 -> 0; matrix products, arithmetic and copies ran while one was open for 26% -> 0% of each run, Pallas kernels for 0% -> 0%
where the time goes in v1:
time: 119 us
  Pallas kernels  113 us (95%)
  local copies, waits for them, and re-layouts  5.72 us (5%)
    pallas_call x1, Pallas kernels, on_device(): pl.pallas_call(kernel, out_shape=(jax.ShapeDtypeStruct((HALF, FF), BF16),...  113 us
    unnamed x7, local copies, waits for them, and re-layouts  5.72 us

profile of v1, /device:TPU:1, one launch (start us, length us, event | category | flops | bytes accessed | tf_op | source)
XLA Modules:
  0.0 119.2 jit_solution(5720025442655520610)
XLA Ops:
  0.6 112.8 %shard_map.67 = (bf16[256,3584]{1,0:T(8,128)(2,1)}, bf16[256,3584]{1,0:T(8,128)(2,1)}, bf16[3584,128]{1,0:T(8,128)(2,1)}) custom-call(bf16[128,2048]{1,0:T(8,128)(2,1)} %bitcast.9, bf16[256,3584]{1,0:T(8,128)(2,1)} %bitcast.7, bf16[256,3584]{1,0:T(8,128)(2,1)} %bitcast.8, bf16[3584,2048]{1,0:T(8,128)(2,1)} %w.1), custom_call_target="tpu_custom_call" | custom-call | flops 15032385536 | bytes 24000000 | tf_op jit(solution)/shard_map/pallas_call | solution.py:465
  113.5 0.0 copy-start
  113.5 3.0 %copy.10 = bf16[1,256,3584]{2,1,0:T(8,128)(2,1)} copy(bf16[1,256,3584]{2,1,0:T(8,128)(2,1)} %bitcast.6) | data formatting | bytes 3670016
  116.4 0.0 copy-done
  116.4 0.0 copy-start.1
  116.4 1.2 %copy.11 = bf16[1,256,3584]{2,1,0:T(8,128)(2,1)} copy(bf16[1,256,3584]{2,1,0:T(8,128)(2,1)S(1)} %bitcast.5) | data formatting | bytes 3670016
  117.7 0.6 copy-done.1
  118.3 0.9 copy.12
Async XLA Ops:
  113.5 3.0 %copy-start = (bf16[256,3584]{1,0:T(8,128)(2,1)S(1)}, bf16[256,3584]{1,0:T(8,128)(2,1)}, u32[]{:S(2)}) copy-start(bf16[256,3584]{1,0:T(8,128)(2,1)} %get-tuple-element.7) | copy-start | bytes 5505028
  116.4 1.8 %copy-start.1 = (bf16[3584,128]{1,0:T(8,128)(2,1)S(1)}, bf16[3584,128]{1,0:T(8,128)(2,1)}, u32[]{:S(2)}) copy-start(bf16[3584,128]{1,0:T(8,128)(2,1)} %get-tuple-element.14) | copy-start | bytes 2752516

commit v2 on v1

--- a/solution.py
+++ b/solution.py
@@ -12,22 +12,25 @@
 HALF = TOK // 2
 ROWS = TOK // 4
 FC = 512
+NC = FF // FC
 HF = FC // 2
-NC = FF // FC
+NU = FF // HF
+NY = 6
+NZ = NU - NY
 BLK = 128
 STEP = 32
 SCALE = float(16 * TOK) ** -0.5
 
 
 def kernel(
-    go, gate, up, w, o_gate, o_up, o_w,
-    g_own, g_pair, g_t, hid, gate_v, up_v, wbuf, ghs, ghr, wout,
+    go, gate, up, w, gate_v, up_v, wout,
+    g_own, g_pair, g_t, hid, wbuf, ghs, ghr,
     zs0, zr0, zs1, zr1, es, er, zkeep,
     as_, ar, ys0, yr0, ys1, yr1, ykeep,
     xo_s, xo_r, xf_s, xf_r, pp_s, pp_r, px_s, px_r, pf_s, pf_r,
     hc_s, hc_r, hp_s, hp_r, hf_s, hf_r,
     z0_s, z0_r, z1_s, z1_r, e_s, e_r, a_s, a_r, y0_s, y0_r, y1_s, y1_r,
-    gh_s, gh_r, ld_g, ld_u, ld_o, ld_w, st_g, st_u, st_w,
+    gh_s, gh_r, ld_g, ld_u, ld_o, ld_w,
 ):
     x, c, q = lax.axis_index("row"), lax.axis_index("col"), lax.axis_index("depth")
     z, y = lax.div(q, 4), lax.rem(q, 4)
@@ -121,17 +124,25 @@
         f = ds(k * FC, FC, FC)
         return pltpu.make_async_copy(src.at[:, f], dst.at[:, f], sem.at[k])
 
-    def hid_view(group, half, k):
-        return hid.at[ds(group * TOK + half * HALF, HALF, HALF), ds(k * FC, FC, FC)]
-
-    def hid_core(k):
-        return send(hid_view(0, c, k), hid_view(0, c, k), hc_s.at[k], hc_r.at[k], core)
-
-    def hid_pair(k):
-        return send(hid_view(0, c, k), hid_view(1, c, k), hp_s.at[k], hp_r.at[k], pair)
-
-    def hid_pass(k):
-        return send(hid_view(1, c, k), hid_view(1, c, k), hf_s.at[k], hf_r.at[k], core)
+    def hid_view(group, u):
+        return hid.at[ds(group * TOK + c * HALF, HALF, HALF), ds(u * HF, HF, HF)]
+
+    def hid_core(u):
+        return send(hid_view(0, u), hid_view(0, u), hc_s.at[u], hc_r.at[u], core)
+
+    def hid_pair(u):
+        return send(hid_view(0, u), hid_view(1, u), hp_s.at[u], hp_r.at[u], pair)
+
+    def hid_pass(u):
+        return send(hid_view(1, u), hid_view(1, u), hf_s.at[u], hf_r.at[u], core)
+
+    def pass_on(u):
+        hid_pair(u).wait_recv()
+        hid_pass(u).start()
+
+    def have_hidden(u):
+        hid_core(u).wait_recv()
+        hid_pass(u).wait_recv()
 
     def make_hidden(k):
         in_copy(k, gate, gate_v, ld_g).wait()
@@ -146,11 +157,18 @@
             return carry
 
         lax.fori_loop(0, HALF // STEP, rows, 0)
-        hid_pair(k).start()
-        hid_core(k).start()
-
-    def dot(rows, k, part):
-        return jnp.dot(rows, hid[:, ds(k * FC + part * HF, HF, HF)], preferred_element_type=F32)
+        for u in (2 * k, 2 * k + 1):
+            hid_pair(u).start()
+            hid_core(u).start()
+
+    def dot(rows, u):
+        return jnp.dot(rows, hid[:, ds(u * HF, HF, HF)], preferred_element_type=F32)
+
+    def unit_z(k):
+        return jnp.maximum(2 * k - 1, 0)
+
+    def unit_y(k):
+        return 2 * k + 2
 
     def of_layer(j):
         return g_t[2 * BLK * j : 2 * BLK * (j + 1), :]
@@ -178,18 +196,20 @@
     def y1(k, way):
         return send(ys1.at[k, way], yr1.at[k, way], y1_s.at[k, way], y1_r.at[k, way], (above, below)[way])
 
-    def stage0(k):
-        part = dot(of_layer(0), k, 1).astype(BF16)
+    def z_stage0(k):
+        part = dot(of_layer(0), unit_z(k)).astype(BF16)
         for half in (0, 1):
             zs0[k, half] = part[:, half * BLK : (half + 1) * BLK]
             z0(k, half).start()
+
+    def y_stage0(k):
         for h in (0, 1):
-            as_[k, 2 * BLK * h : 2 * BLK * (h + 1), :] = dot(of_column(1, h), k, 0).astype(BF16)
+            as_[k, 2 * BLK * h : 2 * BLK * (h + 1), :] = dot(of_column(1, h), unit_y(k)).astype(BF16)
         y_first(k).start()
 
-    def stage1(k):
+    def z_stage1(k):
         for way in (0, 1):
-            part = dot(of_layer(1 + way), k, 1)
+            part = dot(of_layer(1 + way), unit_z(k))
             half = 1 - way
             z0(k, half).wait_recv()
             lo, hi = part[:, :BLK], part[:, BLK:]
@@ -201,7 +221,9 @@
             zs1[k, way, :, :BLK] = lo.astype(BF16)
             zs1[k, way, :, BLK:] = hi.astype(BF16)
             z1(k, way).start()
-        parts = [dot(of_column(0, h), k, 0) for h in (0, 1)]
+
+    def y_stage1(k):
+        parts = [dot(of_column(0, h), unit_y(k)) for h in (0, 1)]
         y_first(k).wait_recv()
         first = parts[0] + ar[k, : 2 * BLK, :].astype(F32)
         far = first[:BLK, :].astype(BF16)
@@ -211,7 +233,16 @@
         ykeep[k, :BLK, :] = first[BLK:, :]
         ykeep[k, BLK:, :] = parts[1] + ar[k, 2 * BLK :, :].astype(F32)
 
-    def stage2(k):
+    def z_stage2(k):
+        part = dot(of_layer(3), unit_z(k))
+        for way in (0, 1):
+            z1(k, way).wait_recv()
+            part = part + zr1[k, way].astype(F32)
+        es[k] = part[BLK:, :].astype(BF16)
+        z_last(k).start()
+        zkeep[k] = part[:BLK, :]
+
+    def y_stage2(k):
         for way in (0, 1):
             half = 1 - way
             y0(k, half).wait_recv()
@@ -224,28 +255,18 @@
             ys1[k, way, :, :BLK] = lo.astype(BF16)
             ys1[k, way, :, BLK:] = hi.astype(BF16)
             y1(k, way).start()
-        part = dot(of_layer(3), k, 1)
-        for way in (0, 1):
-            z1(k, way).wait_recv()
-            part = part + zr1[k, way].astype(F32)
-        es[k] = part[BLK:, :].astype(BF16)
-        z_last(k).start()
-        zkeep[k] = part[:BLK, :]
-
-    def out_copy(k):
-        f = ds(k * FC, FC, FC)
-        return pltpu.make_async_copy(wout.at[f], o_w.at[f], st_w.at[k])
-
-    def stage3(k):
+
+    def z_stage3(k):
+        z_last(k).wait_recv()
+        total = zkeep[k] + er[k].astype(F32)
+        wout[ds(unit_z(k) * HF, HF, HF), :] = (total * SCALE).T.astype(BF16)
+
+    def y_stage3(k):
         total = ykeep[k, 2 * BLK :, :]
         for way in (0, 1):
             y1(k, way).wait_recv()
             total = total + yr1[k, way].astype(F32)
-        wout[ds(k * FC, HF, HF), :] = (total * SCALE).T.astype(BF16)
-        z_last(k).wait_recv()
-        total = zkeep[k] + er[k].astype(F32)
-        wout[ds(k * FC + HF, HF, HF), :] = (total * SCALE).T.astype(BF16)
-        out_copy(k).start()
+        wout[ds(unit_y(k) * HF, HF, HF), :] = (total * SCALE).T.astype(BF16)
 
     def w_copy(k):
         slot = lax.rem(k, 2)
@@ -270,13 +291,6 @@
         @pl.when(k + 2 < NC)
         def _():
             w_copy(k + 2).start()
-
-    def gate_out(k):
-        f = ds(k * FC, FC, FC)
-        return (
-            pltpu.make_async_copy(gate_v.at[:, f], o_gate.at[:, f], st_g.at[k]),
-            pltpu.make_async_copy(up_v.at[:, f], o_up.at[:, f], st_u.at[k]),
-        )
 
     def grad_gate(k):
         gh_send(k).wait_recv()
@@ -293,58 +307,69 @@
             return carry
 
         lax.fori_loop(0, HALF // STEP, rows, 0)
-        for copy in gate_out(k):
-            copy.start()
-
-    def loads(k, carry):
+
+    def loop(lo, hi, step):
+        def run(i, carry):
+            step(i)
+            return carry
+
+        lax.fori_loop(lo, hi, run, 0)
+
+    def load(k):
         in_copy(k, gate, gate_v, ld_g).start()
         in_copy(k, up, up_v, ld_u).start()
-        return carry
+
+    def pair_start(j):
+        for s in (0, 1):
+            pair_send(j, s).start()
 
     own_start(0, 0)
-    for s in (0, 1):
-        pair_send(0, s).start()
-    lax.fori_loop(0, NC, loads, 0)
+    own_start(1, 0)
+    pair_start(0)
+    pair_start(1)
+    loop(0, NC, load)
     own_copy().start()
     w_copy(0).start()
     w_copy(1).start()
 
-    def first_hidden(k, carry):
+    def first_hidden(k):
         make_hidden(k)
 
         @pl.when(k == 0)
         def _():
-            for j in (1, 2, 3):
-                for s in (0, 1):
-                    pair_send(j, s).start()
-
-        return carry
-
-    lax.fori_loop(0, 2, first_hidden, 0)
+            pair_start(2)
+            pair_start(3)
+
+    loop(0, 3, first_hidden)
+
+    def gather(t):
+        @pl.when(t < 4)
+        def _():
+            own_pass(t, 0)
+            for s in (0, 1):
+                pair_send(t, s).wait_recv()
+            for side in (0, 1):
+                pair_direct(t, side).start()
+
+        @pl.when(t < 2)
+        def _():
+            own_start(t + 2, 0)
+
+        @pl.when(t >= 1)
+        def _():
+            for side in (0, 1):
+                pair_direct(t - 1, side).wait_recv()
+                pair_forward(t - 1, side).start()
+
+        @pl.when(t < 4)
+        def _():
+            make_hidden(t + 3)
+
+    loop(0, 5, gather)
+    loop(0, 4, lambda j: own_start(j, 2))
     own_copy().wait()
 
-    def gather(j, carry):
-        @pl.when(j < 3)
-        def _():
-            own_start(j + 1, 0)
-
-        for s in (0, 1):
-            pair_send(j, s).wait_recv()
-        for side in (0, 1):
-            pair_direct(j, side).start()
-        own_pass(j, 0)
-        for side in (0, 1):
-            pair_direct(j, side).wait_recv()
-            pair_forward(j, side).start()
-
-        @pl.when(j == 3)
-        def _():
-            def rest(i, carry):
-                own_start(i, 2)
-                return carry
-
-            lax.fori_loop(0, 4, rest, 0)
-
+    def turn(j):
         own_end(j, 0)
         for side in (0, 1):
             pair_forward(j, side).wait_recv()
@@ -352,84 +377,94 @@
             rows = ds((j * 2 + s) * BLK, BLK, BLK)
             g_t[rows, :TOK] = g_own[:, cols(block_of(j, s))].T
             g_t[rows, TOK:] = g_pair[:, cols(j * 2 + s)].T
-        return carry
-
-    lax.fori_loop(0, 4, gather, 0)
-    hid_pair(0).wait_recv()
-    hid_pass(0).start()
-
-    def body(i, carry):
-        @pl.when(i + 2 < NC)
-        def _():
-            make_hidden(i + 2)
-
+
+        @pl.when(j < 2)
+        def _():
+            pass_on(j)
+            have_hidden(j)
+            z_stage0(j)
+
+        @pl.when(j == 2)
+        def _():
+            z_stage1(0)
+
+    loop(0, 4, turn)
+
+    def body(i):
         @pl.when(i < NC)
         def _():
-            hid_core(i).wait_recv()
-            hid_pass(i).wait_recv()
-            stage0(i)
-
-        @pl.when(jnp.logical_and(i >= 1, i < NC + 1))
-        def _():
-            stage1(i - 1)
-
-        @pl.when(jnp.logical_and(i >= 2, i < NC + 2))
-        def _():
-            stage2(i - 2)
-
-        @pl.when(jnp.logical_and(i >= 3, i < NC + 3))
-        def _():
-            stage3(i - 3)
-
-        @pl.when(i < 4)
-        def _():
-            own_pass(i, 2)
-
-        @pl.when(i == 3)
-        def _():
-            def rest(j, carry):
-                own_end(j, 2)
-                return carry
-
-            lax.fori_loop(0, 4, rest, 0)
-
-        @pl.when(jnp.logical_and(i >= 3, i < NC + 3))
-        def _():
-            grad_hidden(i - 3)
-
-        @pl.when(i >= 4)
-        def _():
-            grad_gate(i - 4)
-
-        @pl.when(i + 1 < NC)
-        def _():
-            hid_pair(i + 1).wait_recv()
-            hid_pass(i + 1).start()
-
-        return carry
-
-    lax.fori_loop(0, NC + 4, body, 0)
-
-    def sent(k, carry):
-        hid_core(k).wait_send()
-        hid_pair(k).wait_send()
-        hid_pass(k).wait_send()
+            pass_on(2 * i)
+            have_hidden(2 * i)
+            y_stage0(i - 1)
+            pass_on(2 * i + 1)
+            have_hidden(2 * i + 1)
+            z_stage0(i + 1)
+
+        @pl.when(i < NZ)
+        def _():
+            z_stage1(i)
+
+        @pl.when(jnp.logical_and(i >= 2, i < NY + 2))
+        def _():
+            y_stage1(i - 2)
+
+        @pl.when(i < NZ + 1)
+        def _():
+            z_stage2(i - 1)
+
+        @pl.when(jnp.logical_and(i >= 3, i < NY + 3))
+        def _():
+            y_stage2(i - 3)
+
+        @pl.when(jnp.logical_and(i >= 2, i < NZ + 2))
+        def _():
+            z_stage3(i - 2)
+
+        @pl.when(jnp.logical_and(i >= 4, i < NY + 4))
+        def _():
+            y_stage3(i - 4)
+
+        @pl.when(i == 1)
+        def _():
+            loop(0, 4, lambda j: own_pass(j, 2))
+
+        @pl.when(i == 2)
+        def _():
+            loop(0, 4, lambda j: own_end(j, 2))
+
+        def products(d):
+            k = 2 * i - 5 + d
+
+            @pl.when(jnp.logical_and(k >= 0, k < NC))
+            def _():
+                grad_hidden(k)
+
+            @pl.when(jnp.logical_and(k >= 2, k < NC + 2))
+            def _():
+                grad_gate(k - 2)
+
+        loop(0, 2, products)
+
+    loop(1, NZ + 2, body)
+
+    def sent(u):
+        hid_core(u).wait_send()
+        hid_pair(u).wait_send()
+        hid_pass(u).wait_send()
+
+    def sent_z(k):
         for i in (0, 1):
             z0(k, i).wait_send()
             z1(k, i).wait_send()
+        z_last(k).wait_send()
+
+    def sent_y(k):
+        for i in (0, 1):
             y0(k, i).wait_send()
             y1(k, i).wait_send()
-        z_last(k).wait_send()
         y_first(k).wait_send()
-        gh_send(k).wait_send()
-        for copy in gate_out(k):
-            copy.wait()
-        out_copy(k).wait()
-        return carry
-
-    lax.fori_loop(0, NC, sent, 0)
-
-    def sent_x(j, carry):
+
+    def sent_x(j):
         for s in range(4):
             for side in (0, 1):
                 own_direct(block_of(j, s), side).wait_send()
@@ -439,9 +474,12 @@
         for side in (0, 1):
             pair_direct(j, side).wait_send()
             pair_forward(j, side).wait_send()
-        return carry
-
-    lax.fori_loop(0, 4, sent_x, 0)
+
+    loop(0, NU, sent)
+    loop(0, NZ, sent_z)
+    loop(0, NY, sent_y)
+    loop(0, NC, lambda k: gh_send(k).wait_send())
+    loop(0, 4, sent_x)
 
 
 def on_device(grad_out, gate_pre, up_pre, down_weight):
@@ -449,31 +487,27 @@
     vmem = lambda *shape: pltpu.VMEM(shape, BF16)
     scratch = [
         vmem(TOK, DM), vmem(TOK, 8 * BLK), vmem(8 * BLK, 2 * TOK), vmem(2 * TOK, FF),
-        vmem(HALF, FF), vmem(HALF, FF), vmem(2, FC, DM), vmem(NC, TOK, FC), vmem(NC, HALF, FC), vmem(FF, BLK),
-        vmem(NC, 2, 2 * BLK, BLK), vmem(NC, 2, 2 * BLK, BLK), vmem(NC, 2, 2 * BLK, HF), vmem(NC, 2, 2 * BLK, HF),
-        vmem(NC, BLK, HF), vmem(NC, BLK, HF), pltpu.VMEM((NC, BLK, HF), F32),
-        vmem(NC, 4 * BLK, HF), vmem(NC, 4 * BLK, HF), vmem(NC, 2, BLK, BLK), vmem(NC, 2, BLK, BLK),
-        vmem(NC, 2, BLK, HF), vmem(NC, 2, BLK, HF), pltpu.VMEM((NC, 3 * BLK, HF), F32),
+        vmem(2, FC, DM), vmem(NC, TOK, FC), vmem(NC, HALF, FC),
+        vmem(NZ, 2, 2 * BLK, BLK), vmem(NZ, 2, 2 * BLK, BLK), vmem(NZ, 2, 2 * BLK, HF), vmem(NZ, 2, 2 * BLK, HF),
+        vmem(NZ, BLK, HF), vmem(NZ, BLK, HF), pltpu.VMEM((NZ, BLK, HF), F32),
+        vmem(NY, 4 * BLK, HF), vmem(NY, 4 * BLK, HF), vmem(NY, 2, BLK, BLK), vmem(NY, 2, BLK, BLK),
+        vmem(NY, 2, BLK, HF), vmem(NY, 2, BLK, HF), pltpu.VMEM((NY, 3 * BLK, HF), F32),
         dma((16, 2)), dma((16, 2)), dma((16, 2)), dma((16, 2)), dma((8,)), dma((8,)),
         dma((4, 2)), dma((4, 2)), dma((4, 2)), dma((4, 2)),
-        dma((NC,)), dma((NC,)), dma((NC,)), dma((NC,)), dma((NC,)), dma((NC,)),
-        dma((NC, 2)), dma((NC, 2)), dma((NC, 2)), dma((NC, 2)), dma((NC,)), dma((NC,)),
-        dma((NC,)), dma((NC,)), dma((NC, 2)), dma((NC, 2)), dma((NC, 2)), dma((NC, 2)),
-        dma((NC,)), dma((NC,)), dma((NC,)), dma((NC,)), dma, dma((2,)), dma((NC,)), dma((NC,)), dma((NC,)),
+        dma((NU,)), dma((NU,)), dma((NU,)), dma((NU,)), dma((NU,)), dma((NU,)),
+        dma((NZ, 2)), dma((NZ, 2)), dma((NZ, 2)), dma((NZ, 2)), dma((NZ,)), dma((NZ,)),
+        dma((NY,)), dma((NY,)), dma((NY, 2)), dma((NY, 2)), dma((NY, 2)), dma((NY, 2)),
+        dma((NC,)), dma((NC,)), dma((NC,)), dma((NC,)), dma, dma((2,)),
     ]
     anywhere = pl.BlockSpec(memory_space=pl.ANY)
     grad_gate, grad_up, grad_weight = pl.pallas_call(
         kernel,
-        out_shape=(
-            jax.ShapeDtypeStruct((HALF, FF), BF16),
-            jax.ShapeDtypeStruct((HALF, FF), BF16),
-            jax.ShapeDtypeStruct((FF, BLK), BF16),
-        ),
+        out_shape=(pltpu.VMEM((HALF, FF), BF16), pltpu.VMEM((HALF, FF), BF16), pltpu.VMEM((FF, BLK), BF16)),
         in_specs=[anywhere] * 4,
-        out_specs=(anywhere,) * 3,
+        out_specs=(pl.BlockSpec(memory_space=pltpu.VMEM),) * 3,
         scratch_shapes=scratch,
         compiler_params=pltpu.CompilerParams(
-            collective_id=0, has_side_effects=True, vmem_limit_bytes=60 * 2**20
+            collective_id=0, has_side_effects=True, vmem_limit_bytes=48 * 2**20
         ),
         cost_estimate=pl.CostEstimate(flops=4 * TOK * FF * DM, bytes_accessed=24 * 10**6, transcendentals=2 * HALF * FF),
     )(grad_out[0], gate_pre[0], up_pre[0], down_weight)

time: 119 us -> 100 us (0.84); the launches traced: 119 us -> 98.5 us
  Pallas kernels: 113 us -> 93.4 us
  local copies, waits for them, and re-layouts: 5.72 us -> 4.42 us
    pallas_call x1, Pallas kernels: 113 us -> 93.4 us  [on_device(): pl.pallas_call(kernel, out_shape=(pltpu.VMEM((HALF, FF), BF16), pltpu.VME...]
    unnamed x7 -> x5, local copies, waits for them, and re-layouts: 5.72 us -> 4.42 us
where the time goes in v2:
time: 100 us; the launch traced here: 98.5 us
  Pallas kernels  93.4 us (93%)
  local copies, waits for them, and re-layouts  4.42 us (4%)
    pallas_call x1, Pallas kernels, on_device(): pl.pallas_call(kernel, out_shape=(pltpu.VMEM((HALF, FF), BF16), pltpu.VME...  93.4 us
    unnamed x5, local copies, waits for them, and re-layouts  4.42 us

profile of v2, /device:TPU:1, one launch (start us, length us, event | category | flops | bytes accessed | tf_op | source)
XLA Modules:
  0.0 98.5 jit_solution(13836452651896794122)
XLA Ops:
  0.6 0.0 copy-start
  0.6 1.0 %copy-done = bf16[1,128,2048]{2,1,0:T(8,128)(2,1)S(1)} copy-done((bf16[1,128,2048]{2,1,0:T(8,128)(2,1)S(1)}, bf16[1,128,2048]{2,1,0:T(8,128)(2,1)}, u32[]{:S(2)}) %copy-start) | copy-done | bytes 524312
  1.7 93.4 %shard_map.67 = (bf16[256,3584]{1,0:T(8,128)(2,1)S(1)}, bf16[256,3584]{1,0:T(8,128)(2,1)S(1)}, bf16[3584,128]{1,0:T(8,128)(2,1)S(1)}) custom-call(bf16[128,2048]{1,0:T(8,128)(2,1)S(1)} %bitcast.7, bf16[256,3584]{1,0:T(8,128)(2,1)} %bitcast.8, bf16[256,3584]{1,0:T(8,128)(2,1)} %bitcast.9, bf16[3584,2048]{1,0:T(8,128)(2,1)} %w.1), custom_call_target="tpu_custom_call" | custom-call | flops 15032385536 | bytes 24000000 | tf_op jit(solution)/shard_map/pallas_call | solution.py:503
  95.1 1.2 %copy.10 = bf16[1,256,3584]{2,1,0:T(8,128)(2,1)} copy(bf16[1,256,3584]{2,1,0:T(8,128)(2,1)S(1)} %bitcast.6) | data formatting | bytes 3670016
  96.4 1.2 %copy.11 = bf16[1,256,3584]{2,1,0:T(8,128)(2,1)} copy(bf16[1,256,3584]{2,1,0:T(8,128)(2,1)S(1)} %bitcast.5) | data formatting | bytes 3670016
  97.6 0.9 copy.12
Async XLA Ops:
  0.6 1.0 %copy-start = (bf16[1,128,2048]{2,1,0:T(8,128)(2,1)S(1)}, bf16[1,128,2048]{2,1,0:T(8,128)(2,1)}, u32[]{:S(2)}) copy-start(bf16[1,128,2048]{2,1,0:T(8,128)(2,1)} %param.4) | copy-start | bytes 1572868

commit v3 on v2

--- a/solution.py
+++ b/solution.py
@@ -15,11 +15,15 @@
 NC = FF // FC
 HF = FC // 2
 NU = FF // HF
-NY = 6
+NY = 5
 NZ = NU - NY
 BLK = 128
 STEP = 32
 SCALE = float(16 * TOK) ** -0.5
+
+
+def sigmoid(v):
+    return 0.5 * jnp.tanh(0.5 * v) + 0.5
 
 
 def kernel(
@@ -48,8 +52,6 @@
     barrier = pltpu.get_barrier_semaphore()
     for other in (core, right, left, pair, across, above, below):
         pl.semaphore_signal(barrier, inc=1, device_id=other, device_id_type=MESH)
-    pl.semaphore_wait(barrier, 7)
-
     def send(src, dst, ss, rs, device):
         return pltpu.make_async_remote_copy(
             src_ref=src, dst_ref=dst, send_sem=ss, recv_sem=rs, device_id=device, device_id_type=MESH
@@ -153,7 +155,7 @@
             r = ds(i * STEP, STEP, STEP)
             g = gate_v[r, f].astype(F32)
             u = up_v[r, f].astype(F32)
-            hid[ds(c * HALF + i * STEP, STEP, STEP), f] = (g * (1.0 / (1.0 + jnp.exp(-g))) * u).astype(BF16)
+            hid[ds(c * HALF + i * STEP, STEP, STEP), f] = (g * sigmoid(g) * u).astype(BF16)
             return carry
 
         lax.fori_loop(0, HALF // STEP, rows, 0)
@@ -165,10 +167,10 @@
         return jnp.dot(rows, hid[:, ds(u * HF, HF, HF)], preferred_element_type=F32)
 
     def unit_z(k):
-        return jnp.maximum(2 * k - 1, 0)
+        return jnp.maximum(k, 2 * k - 3)
 
     def unit_y(k):
-        return 2 * k + 2
+        return 2 * k + 4
 
     def of_layer(j):
         return g_t[2 * BLK * j : 2 * BLK * (j + 1), :]
@@ -301,151 +303,12 @@
             g = gate_v[r, f].astype(F32)
             u = up_v[r, f].astype(F32)
             grad = ghs[k, ds(c * HALF + i * STEP, STEP, STEP), :].astype(F32) + ghr[k, r, :].astype(F32)
-            sig = 1.0 / (1.0 + jnp.exp(-g))
+            sig = sigmoid(g)
             gate_v[r, f] = (grad * u * (sig * (1.0 + g * (1.0 - sig)))).astype(BF16)
             up_v[r, f] = (grad * (g * sig)).astype(BF16)
             return carry
 
         lax.fori_loop(0, HALF // STEP, rows, 0)
-
-    def loop(lo, hi, step):
-        def run(i, carry):
-            step(i)
-            return carry
-
-        lax.fori_loop(lo, hi, run, 0)
-
-    def load(k):
-        in_copy(k, gate, gate_v, ld_g).start()
-        in_copy(k, up, up_v, ld_u).start()
-
-    def pair_start(j):
-        for s in (0, 1):
-            pair_send(j, s).start()
-
-    own_start(0, 0)
-    own_start(1, 0)
-    pair_start(0)
-    pair_start(1)
-    loop(0, NC, load)
-    own_copy().start()
-    w_copy(0).start()
-    w_copy(1).start()
-
-    def first_hidden(k):
-        make_hidden(k)
-
-        @pl.when(k == 0)
-        def _():
-            pair_start(2)
-            pair_start(3)
-
-    loop(0, 3, first_hidden)
-
-    def gather(t):
-        @pl.when(t < 4)
-        def _():
-            own_pass(t, 0)
-            for s in (0, 1):
-                pair_send(t, s).wait_recv()
-            for side in (0, 1):
-                pair_direct(t, side).start()
-
-        @pl.when(t < 2)
-        def _():
-            own_start(t + 2, 0)
-
-        @pl.when(t >= 1)
-        def _():
-            for side in (0, 1):
-                pair_direct(t - 1, side).wait_recv()
-                pair_forward(t - 1, side).start()
-
-        @pl.when(t < 4)
-        def _():
-            make_hidden(t + 3)
-
-    loop(0, 5, gather)
-    loop(0, 4, lambda j: own_start(j, 2))
-    own_copy().wait()
-
-    def turn(j):
-        own_end(j, 0)
-        for side in (0, 1):
-            pair_forward(j, side).wait_recv()
-        for s in (0, 1):
-            rows = ds((j * 2 + s) * BLK, BLK, BLK)
-            g_t[rows, :TOK] = g_own[:, cols(block_of(j, s))].T
-            g_t[rows, TOK:] = g_pair[:, cols(j * 2 + s)].T
-
-        @pl.when(j < 2)
-        def _():
-            pass_on(j)
-            have_hidden(j)
-            z_stage0(j)
-
-        @pl.when(j == 2)
-        def _():
-            z_stage1(0)
-
-    loop(0, 4, turn)
-
-    def body(i):
-        @pl.when(i < NC)
-        def _():
-            pass_on(2 * i)
-            have_hidden(2 * i)
-            y_stage0(i - 1)
-            pass_on(2 * i + 1)
-            have_hidden(2 * i + 1)
-            z_stage0(i + 1)
-
-        @pl.when(i < NZ)
-        def _():
-            z_stage1(i)
-
-        @pl.when(jnp.logical_and(i >= 2, i < NY + 2))
-        def _():
-            y_stage1(i - 2)
-
-        @pl.when(i < NZ + 1)
-        def _():
-            z_stage2(i - 1)
-
-        @pl.when(jnp.logical_and(i >= 3, i < NY + 3))
-        def _():
-            y_stage2(i - 3)
-
-        @pl.when(jnp.logical_and(i >= 2, i < NZ + 2))
-        def _():
-            z_stage3(i - 2)
-
-        @pl.when(jnp.logical_and(i >= 4, i < NY + 4))
-        def _():
-            y_stage3(i - 4)
-
-        @pl.when(i == 1)
-        def _():
-            loop(0, 4, lambda j: own_pass(j, 2))
-
-        @pl.when(i == 2)
-        def _():
-            loop(0, 4, lambda j: own_end(j, 2))
-
-        def products(d):
-            k = 2 * i - 5 + d
-
-            @pl.when(jnp.logical_and(k >= 0, k < NC))
-            def _():
-                grad_hidden(k)
-
-            @pl.when(jnp.logical_and(k >= 2, k < NC + 2))
-            def _():
-                grad_gate(k - 2)
-
-        loop(0, 2, products)
-
-    loop(1, NZ + 2, body)
 
     def sent(u):
         hid_core(u).wait_send()
@@ -475,11 +338,174 @@
             pair_direct(j, side).wait_send()
             pair_forward(j, side).wait_send()
 
-    loop(0, NU, sent)
+    def loop(lo, hi, step):
+        def run(i, carry):
+            step(i)
+            return carry
+
+        lax.fori_loop(lo, hi, run, 0)
+
+    def load(k):
+        in_copy(k, gate, gate_v, ld_g).start()
+        in_copy(k, up, up_v, ld_u).start()
+
+    def pair_start(j):
+        for s in (0, 1):
+            pair_send(j, s).start()
+
+    loop(0, NC, load)
+    own_copy().start()
+    w_copy(0).start()
+    w_copy(1).start()
+    pl.semaphore_wait(barrier, 7)
+    own_start(0, 0)
+    pair_start(0)
+    own_start(1, 0)
+    pair_start(1)
+
+    make_hidden(0)
+    pair_start(2)
+    pair_start(3)
+    own_copy().wait()
+
+    def turn(j):
+        own_end(j, 0)
+        for side in (0, 1):
+            pair_forward(j, side).wait_recv()
+        for s in (0, 1):
+            rows = ds((j * 2 + s) * BLK, BLK, BLK)
+            g_t[rows, :TOK] = g_own[:, cols(block_of(j, s))].T
+            g_t[rows, TOK:] = g_pair[:, cols(j * 2 + s)].T
+
+    def gather(t):
+        make_hidden(t + 1)
+
+        @pl.when(jnp.logical_and(t >= 3, t < 5))
+        def _():
+            have_hidden(t - 3)
+            z_stage0(t - 3)
+
+        @pl.when(t >= 2)
+        def _():
+            turn(t - 2)
+
+        @pl.when(t == 4)
+        def _():
+            loop(0, 2, z_stage1)
+
+        @pl.when(jnp.logical_and(t >= 1, t < 5))
+        def _():
+            for side in (0, 1):
+                pair_direct(t - 1, side).wait_recv()
+                pair_forward(t - 1, side).start()
+
+        @pl.when(t == 4)
+        def _():
+            loop(0, 4, lambda j: own_start(j, 2))
+
+        @pl.when(t < 4)
+        def _():
+            for s in (0, 1):
+                pair_send(t, s).wait_recv()
+            for side in (0, 1):
+                pair_direct(t, side).start()
+
+        @pl.when(jnp.logical_and(t >= 1, t < 3))
+        def _():
+            pass_on(t - 1)
+
+        @pl.when(t < 2)
+        def _():
+            own_start(t + 2, 0)
+
+        @pl.when(t < 4)
+        def _():
+            own_pass(t, 0)
+
+    loop(0, NC - 1, gather)
+
+    def products(k, on):
+        @pl.when(on)
+        def _():
+            grad_hidden(k)
+
+    def gates(k, on):
+        @pl.when(on)
+        def _():
+            grad_gate(k)
+
+    def body(i):
+        @pl.when(i < NC)
+        def _():
+            pass_on(2 * i)
+            pass_on(2 * i + 1)
+
+        @pl.when(i == 2)
+        def _():
+            loop(0, 4, lambda j: own_pass(j, 2))
+
+        @pl.when(i == 3)
+        def _():
+            loop(0, 4, lambda j: own_end(j, 2))
+
+        def early(d):
+            products(jnp.where(i < 5, 2 * i - 6, i - 1) + d, jnp.logical_and(i >= 3, i < jnp.where(d == 0, 8, 5)))
+
+        loop(0, 2, early)
+
+        @pl.when(i < NC)
+        def _():
+            have_hidden(2 * i + 1)
+            z_stage0(i + 2)
+            have_hidden(2 * i)
+
+            @pl.when(i == 1)
+            def _():
+                z_stage0(2)
+
+            @pl.when(i >= 2)
+            def _():
+                y_stage0(i - 2)
+
+        @pl.when(jnp.logical_and(i >= 2, i < NC + 1))
+        def _():
+            loop(jnp.where(i == 2, 2, i + 1), i + 2, z_stage1)
+
+        @pl.when(jnp.logical_and(i != 2, i < NC + 2))
+        def _():
+            loop(jnp.where(i == 1, 0, jnp.where(i == 3, 2, i)), i + 1, z_stage2)
+
+        @pl.when(jnp.logical_and(i >= 3, i < NY + 3))
+        def _():
+            y_stage1(i - 3)
+
+        @pl.when(jnp.logical_and(i >= 4, i < NY + 4))
+        def _():
+            y_stage2(i - 4)
+
+        def late(d):
+            gates(jnp.where(i < 6, 2 * i - 8, i - 2) + d, jnp.logical_and(i >= 4, i < jnp.where(d == 0, 9, 6)))
+
+        loop(0, 2, late)
+
+        @pl.when(jnp.logical_and(i >= 2, i != 3))
+        def _():
+            loop(jnp.where(i == 2, 0, jnp.where(i == 4, 2, i - 1)), i, z_stage3)
+
+        @pl.when(i >= 5)
+        def _():
+            y_stage3(i - 5)
+
+        @pl.when(i == NC + 1)
+        def _():
+            loop(0, NU, sent)
+            loop(0, NC, lambda k: gh_send(k).wait_send())
+            loop(0, 4, sent_x)
+
+    loop(1, NC + 3, body)
+
     loop(0, NZ, sent_z)
     loop(0, NY, sent_y)
-    loop(0, NC, lambda k: gh_send(k).wait_send())
-    loop(0, 4, sent_x)
 
 
 def on_device(grad_out, gate_pre, up_pre, down_weight):
@@ -503,7 +529,7 @@
     grad_gate, grad_up, grad_weight = pl.pallas_call(
         kernel,
         out_shape=(pltpu.VMEM((HALF, FF), BF16), pltpu.VMEM((HALF, FF), BF16), pltpu.VMEM((FF, BLK), BF16)),
-        in_specs=[anywhere] * 4,
+        in_specs=[pl.BlockSpec(memory_space=pltpu.HBM)] + [anywhere] * 3,
         out_specs=(pl.BlockSpec(memory_space=pltpu.VMEM),) * 3,
         scratch_shapes=scratch,
         compiler_params=pltpu.CompilerParams(

time: 100 us -> 91.4 us (0.914); the launches traced: 98.5 us -> 91.3 us
  Pallas kernels: 93.4 us -> 86.2 us
    pallas_call x1, Pallas kernels: 93.4 us -> 86.2 us  [on_device(): pl.pallas_call(kernel, out_shape=(pltpu.VMEM((HALF, FF), BF16), pltpu.VME...]
where the time goes in v3:
time: 91.4 us; the launch traced here: 91.3 us
  Pallas kernels  86.2 us (94%)
  local copies, waits for them, and re-layouts  4.42 us (5%)
    pallas_call x1, Pallas kernels, on_device(): pl.pallas_call(kernel, out_shape=(pltpu.VMEM((HALF, FF), BF16), pltpu.VME...  86.2 us
    unnamed x5, local copies, waits for them, and re-layouts  4.42 us

profile of v3, /device:TPU:1, one launch (start us, length us, event | category | flops | bytes accessed | tf_op | source)
XLA Modules:
  0.0 91.3 jit_solution(3274041403873569854)
XLA Ops:
  0.6 0.0 copy-start
  0.6 1.0 %copy-done = bf16[1,128,2048]{2,1,0:T(8,128)(2,1)S(1)} copy-done((bf16[1,128,2048]{2,1,0:T(8,128)(2,1)S(1)}, bf16[1,128,2048]{2,1,0:T(8,128)(2,1)}, u32[]{:S(2)}) %copy-start) | copy-done | bytes 524312
  1.7 86.2 %shard_map.67 = (bf16[256,3584]{1,0:T(8,128)(2,1)S(1)}, bf16[256,3584]{1,0:T(8,128)(2,1)S(1)}, bf16[3584,128]{1,0:T(8,128)(2,1)S(1)}) custom-call(bf16[128,2048]{1,0:T(8,128)(2,1)S(1)} %bitcast.7, bf16[256,3584]{1,0:T(8,128)(2,1)} %bitcast.8, bf16[256,3584]{1,0:T(8,128)(2,1)} %bitcast.9, bf16[3584,2048]{1,0:T(8,128)(2,1)} %w.1), custom_call_target="tpu_custom_call" | custom-call | flops 15032385536 | bytes 24000000 | tf_op jit(solution)/shard_map/pallas_call | solution.py:529
  87.9 1.2 %copy.10 = bf16[1,256,3584]{2,1,0:T(8,128)(2,1)} copy(bf16[1,256,3584]{2,1,0:T(8,128)(2,1)S(1)} %bitcast.6) | data formatting | bytes 3670016
  89.1 1.2 %copy.11 = bf16[1,256,3584]{2,1,0:T(8,128)(2,1)} copy(bf16[1,256,3584]{2,1,0:T(8,128)(2,1)S(1)} %bitcast.5) | data formatting | bytes 3670016
  90.3 0.9 %copy.12 = bf16[3584,128]{1,0:T(8,128)(2,1)} copy(bf16[3584,128]{1,0:T(8,128)(2,1)S(1)} %get-tuple-element.11) | data formatting | bytes 1835008
Async XLA Ops:
  0.6 1.0 %copy-start = (bf16[1,128,2048]{2,1,0:T(8,128)(2,1)S(1)}, bf16[1,128,2048]{2,1,0:T(8,128)(2,1)}, u32[]{:S(2)}) copy-start(bf16[1,128,2048]{2,1,0:T(8,128)(2,1)} %param.4) | copy-start | bytes 1572868

commit v4 on v3

--- a/solution.py
+++ b/solution.py
@@ -366,6 +366,7 @@
     make_hidden(0)
     pair_start(2)
     pair_start(3)
+    loop(1, 5, make_hidden)
     own_copy().wait()
 
     def turn(j):
@@ -378,12 +379,9 @@
             g_t[rows, TOK:] = g_pair[:, cols(j * 2 + s)].T
 
     def gather(t):
-        make_hidden(t + 1)
-
-        @pl.when(jnp.logical_and(t >= 3, t < 5))
-        def _():
-            have_hidden(t - 3)
-            z_stage0(t - 3)
+        @pl.when(jnp.logical_and(t >= 2, t < 4))
+        def _():
+            pass_on(t - 2)
 
         @pl.when(t >= 2)
         def _():
@@ -410,10 +408,6 @@
             for side in (0, 1):
                 pair_direct(t, side).start()
 
-        @pl.when(jnp.logical_and(t >= 1, t < 3))
-        def _():
-            pass_on(t - 1)
-
         @pl.when(t < 2)
         def _():
             own_start(t + 2, 0)
@@ -422,7 +416,16 @@
         def _():
             own_pass(t, 0)
 
-    loop(0, NC - 1, gather)
+        @pl.when(jnp.logical_and(t >= 2, t < 4))
+        def _():
+            have_hidden(t - 2)
+            z_stage0(t - 2)
+
+        @pl.when(t + 5 < NC)
+        def _():
+            make_hidden(t + 5)
+
+    loop(0, 6, gather)
 
     def products(k, on):
         @pl.when(on)
@@ -448,15 +451,11 @@
         def _():
             loop(0, 4, lambda j: own_end(j, 2))
 
-        def early(d):
-            products(jnp.where(i < 5, 2 * i - 6, i - 1) + d, jnp.logical_and(i >= 3, i < jnp.where(d == 0, 8, 5)))
-
-        loop(0, 2, early)
+        products(2 * i - 6, jnp.logical_and(i >= 3, i < 7))
+        gates(2 * i - 8, jnp.logical_and(i >= 4, i < 8))
 
         @pl.when(i < NC)
         def _():
-            have_hidden(2 * i + 1)
-            z_stage0(i + 2)
             have_hidden(2 * i)
 
             @pl.when(i == 1)
@@ -467,30 +466,32 @@
             def _():
                 y_stage0(i - 2)
 
+            have_hidden(2 * i + 1)
+            z_stage0(i + 2)
+
         @pl.when(jnp.logical_and(i >= 2, i < NC + 1))
         def _():
             loop(jnp.where(i == 2, 2, i + 1), i + 2, z_stage1)
 
+        products(2 * i - 5, jnp.logical_and(i >= 3, i < 6))
+
+        @pl.when(jnp.logical_and(i >= 3, i < NY + 3))
+        def _():
+            y_stage1(i - 3)
+
         @pl.when(jnp.logical_and(i != 2, i < NC + 2))
         def _():
             loop(jnp.where(i == 1, 0, jnp.where(i == 3, 2, i)), i + 1, z_stage2)
 
-        @pl.when(jnp.logical_and(i >= 3, i < NY + 3))
-        def _():
-            y_stage1(i - 3)
-
         @pl.when(jnp.logical_and(i >= 4, i < NY + 4))
         def _():
             y_stage2(i - 4)
 
-        def late(d):
-            gates(jnp.where(i < 6, 2 * i - 8, i - 2) + d, jnp.logical_and(i >= 4, i < jnp.where(d == 0, 9, 6)))
-
-        loop(0, 2, late)
-
         @pl.when(jnp.logical_and(i >= 2, i != 3))
         def _():
             loop(jnp.where(i == 2, 0, jnp.where(i == 4, 2, i - 1)), i, z_stage3)
+
+        gates(2 * i - 7, jnp.logical_and(i >= 4, i < 7))
 
         @pl.when(i >= 5)
         def _():
@@ -506,6 +507,19 @@
 
     loop(0, NZ, sent_z)
     loop(0, NY, sent_y)
+
+
+def write_out(gate_v, up_v, weight_v, o_gate, o_up, o_weight, sems):
+    copies = []
+    for src, dst in ((gate_v, o_gate), (up_v, o_up), (weight_v, o_weight)):
+        rows = src.shape[0] // 2
+        for part in (0, 1):
+            r = pl.ds(part * rows, rows)
+            copies.append(pltpu.make_async_copy(src.at[r], dst.at[r], sems.at[len(copies)]))
+    for copy in copies:
+        copy.start()
+    for copy in copies:
+        copy.wait()
 
 
 def on_device(grad_out, gate_pre, up_pre, down_weight):
@@ -526,7 +540,7 @@
         dma((NC,)), dma((NC,)), dma((NC,)), dma((NC,)), dma, dma((2,)),
     ]
     anywhere = pl.BlockSpec(memory_space=pl.ANY)
-    grad_gate, grad_up, grad_weight = pl.pallas_call(
+    results = pl.pallas_call(
         kernel,
         out_shape=(pltpu.VMEM((HALF, FF), BF16), pltpu.VMEM((HALF, FF), BF16), pltpu.VMEM((FF, BLK), BF16)),
         in_specs=[pl.BlockSpec(memory_space=pltpu.HBM)] + [anywhere] * 3,
@@ -536,7 +550,15 @@
             collective_id=0, has_side_effects=True, vmem_limit_bytes=48 * 2**20
         ),
         cost_estimate=pl.CostEstimate(flops=4 * TOK * FF * DM, bytes_accessed=24 * 10**6, transcendentals=2 * HALF * FF),
-    )(grad_out[0], gate_pre[0], up_pre[0], down_weight)
+    )(pltpu.with_memory_space_constraint(grad_out[0], pltpu.HBM), gate_pre[0], up_pre[0], down_weight)
+    grad_gate, grad_up, grad_weight = pl.pallas_call(
+        write_out,
+        out_shape=tuple(jax.ShapeDtypeStruct(r.shape, r.dtype) for r in results),
+        in_specs=[pl.BlockSpec(memory_space=pltpu.VMEM)] * 3,
+        out_specs=(anywhere,) * 3,
+        scratch_shapes=[dma((6,))],
+        compiler_params=pltpu.CompilerParams(vmem_limit_bytes=2**20),
+    )(*(pltpu.with_memory_space_constraint(r, pltpu.VMEM) for r in results))
     return grad_gate[None], grad_up[None], grad_weight
 
 

time: 91.4 us -> 88.6 us (0.969)
  local copies, waits for them, and re-layouts: 4.42 us -> 0 us
  Pallas kernels: 86.2 us -> 87.9 us
    unnamed x5 -> x0, local copies, waits for them, and re-layouts: 4.42 us -> none
    pallas_call x0 -> x1, Pallas kernels: none -> 2.18 us  [on_device(): pl.pallas_call(write_out, out_shape=tuple((jax.ShapeDtypeStruct(r.shape,...]
where the time goes in v4:
time: 88.6 us; the launch traced here: 88.5 us
  Pallas kernels  87.9 us (99%)
    pallas_call x1, Pallas kernels, on_device(): pl.pallas_call(kernel, out_shape=(pltpu.VMEM((HALF, FF), BF16), pltpu.VME...  85.7 us
    pallas_call x1, Pallas kernels, on_device(): pl.pallas_call(write_out, out_shape=tuple((jax.ShapeDtypeStruct(r.shape,...  2.18 us

profile of v4, /device:TPU:1, one launch (start us, length us, event | category | flops | bytes accessed | tf_op | source)
XLA Modules:
  0.0 88.5 jit_solution(6814028845767682292)
XLA Ops:
  0.6 85.7 %shard_map.67 = (bf16[256,3584]{1,0:T(8,128)(2,1)S(1)}, bf16[256,3584]{1,0:T(8,128)(2,1)S(1)}, bf16[3584,128]{1,0:T(8,128)(2,1)S(1)}) custom-call(bf16[128,2048]{1,0:T(8,128)(2,1)} %bitcast.9, bf16[256,3584]{1,0:T(8,128)(2,1)} %bitcast.5, bf16[256,3584]{1,0:T(8,128)(2,1)} %bitcast.6, bf16[3584,2048]{1,0:T(8,128)(2,1)} %w.1), custom_call_target="tpu_custom_call" | custom-call | flops 15032385536 | bytes 24000000 | tf_op jit(solution)/shard_map/pallas_call | solution.py:543
  86.3 2.2 %shard_map.68 = (bf16[256,3584]{1,0:T(8,128)(2,1)}, bf16[256,3584]{1,0:T(8,128)(2,1)}, bf16[3584,128]{1,0:T(8,128)(2,1)}) custom-call(bf16[256,3584]{1,0:T(8,128)(2,1)S(1)} %get-tuple-element.9.gate_v, bf16[256,3584]{1,0:T(8,128)(2,1)S(1)} %get-tuple-element.10.up_v, bf16[3584,128]{1,0:T(8,128)(2,1)S(1)} %get-tuple-element.11.weight_v), custom_call_target="tpu_custom_call" | custom-call | tf_op jit(solution)/shard_map/pallas_call | solution.py:554

commit v5 on v4

--- a/solution.py
+++ b/solution.py
@@ -441,18 +441,34 @@
         @pl.when(i < NC)
         def _():
             pass_on(2 * i)
+
+        @pl.when(i == 2)
+        def _():
+            loop(0, 4, lambda j: own_pass(j, 2))
+
+        @pl.when(i == 3)
+        def _():
+            loop(0, 4, lambda j: own_end(j, 2))
+
+        products(jnp.where(i == 3, 0, i - 2), jnp.logical_and(i >= 3, i < NC + 2))
+
+        @pl.when(i < NC)
+        def _():
             pass_on(2 * i + 1)
 
-        @pl.when(i == 2)
-        def _():
-            loop(0, 4, lambda j: own_pass(j, 2))
-
-        @pl.when(i == 3)
-        def _():
-            loop(0, 4, lambda j: own_end(j, 2))
-
-        products(2 * i - 6, jnp.logical_and(i >= 3, i < 7))
-        gates(2 * i - 8, jnp.logical_and(i >= 4, i < 8))
+        gates(0, i == 4)
+
+        @pl.when(jnp.logical_and(i >= 4, i < NY + 4))
+        def _():
+            y_stage1(i - 4)
+
+        @pl.when(jnp.logical_and(i >= 5, i < NY + 5))
+        def _():
+            y_stage2(i - 5)
+
+        @pl.when(i >= 7)
+        def _():
+            y_stage3(i - 7)
 
         @pl.when(i < NC)
         def _():
@@ -466,44 +482,34 @@
             def _():
                 y_stage0(i - 2)
 
+        products(1, i == 3)
+
+        @pl.when(i < NC)
+        def _():
             have_hidden(2 * i + 1)
             z_stage0(i + 2)
 
+        gates(i - 3, jnp.logical_and(i >= 4, i < NC + 3))
+
+        @pl.when(jnp.logical_and(jnp.logical_and(i >= 3, i != 4), i < NC + 4))
+        def _():
+            loop(jnp.where(i == 3, 0, jnp.where(i == 5, 2, i - 2)), i - 1, z_stage3)
+
         @pl.when(jnp.logical_and(i >= 2, i < NC + 1))
         def _():
             loop(jnp.where(i == 2, 2, i + 1), i + 2, z_stage1)
 
-        products(2 * i - 5, jnp.logical_and(i >= 3, i < 6))
-
-        @pl.when(jnp.logical_and(i >= 3, i < NY + 3))
-        def _():
-            y_stage1(i - 3)
-
         @pl.when(jnp.logical_and(i != 2, i < NC + 2))
         def _():
             loop(jnp.where(i == 1, 0, jnp.where(i == 3, 2, i)), i + 1, z_stage2)
 
-        @pl.when(jnp.logical_and(i >= 4, i < NY + 4))
-        def _():
-            y_stage2(i - 4)
-
-        @pl.when(jnp.logical_and(i >= 2, i != 3))
-        def _():
-            loop(jnp.where(i == 2, 0, jnp.where(i == 4, 2, i - 1)), i, z_stage3)
-
-        gates(2 * i - 7, jnp.logical_and(i >= 4, i < 7))
-
-        @pl.when(i >= 5)
-        def _():
-            y_stage3(i - 5)
-
-        @pl.when(i == NC + 1)
+        @pl.when(i == NC + 2)
         def _():
             loop(0, NU, sent)
             loop(0, NC, lambda k: gh_send(k).wait_send())
             loop(0, 4, sent_x)
 
-    loop(1, NC + 3, body)
+    loop(1, NC + 5, body)
 
     loop(0, NZ, sent_z)
     loop(0, NY, sent_y)
@@ -512,8 +518,8 @@
 def write_out(gate_v, up_v, weight_v, o_gate, o_up, o_weight, sems):
     copies = []
     for src, dst in ((gate_v, o_gate), (up_v, o_up), (weight_v, o_weight)):
-        rows = src.shape[0] // 2
-        for part in (0, 1):
+        rows = src.shape[0] // 4
+        for part in range(4):
             r = pl.ds(part * rows, rows)
             copies.append(pltpu.make_async_copy(src.at[r], dst.at[r], sems.at[len(copies)]))
     for copy in copies:
@@ -556,7 +562,7 @@
         out_shape=tuple(jax.ShapeDtypeStruct(r.shape, r.dtype) for r in results),
         in_specs=[pl.BlockSpec(memory_space=pltpu.VMEM)] * 3,
         out_specs=(anywhere,) * 3,
-        scratch_shapes=[dma((6,))],
+        scratch_shapes=[dma((12,))],
         compiler_params=pltpu.CompilerParams(vmem_limit_bytes=2**20),
     )(*(pltpu.with_memory_space_constraint(r, pltpu.VMEM) for r in results))
     return grad_gate[None], grad_up[None], grad_weight

time: 88.6 us -> 88.2 us (level)
  Pallas kernels: 87.9 us -> 86.9 us
    pallas_call x1, Pallas kernels: 85.7 us -> 84.7 us  [on_device(): pl.pallas_call(kernel, out_shape=(pltpu.VMEM((HALF, FF), BF16), pltpu.VME...]
where the time goes in v5:
time: 88.2 us; the launch traced here: 87.5 us
  Pallas kernels  86.9 us (99%)
    pallas_call x1, Pallas kernels, on_device(): pl.pallas_call(kernel, out_shape=(pltpu.VMEM((HALF, FF), BF16), pltpu.VME...  84.7 us
    pallas_call x1, Pallas kernels, on_device(): pl.pallas_call(write_out, out_shape=tuple((jax.ShapeDtypeStruct(r.shape,...  2.23 us

profile of v5, /device:TPU:1, one launch (start us, length us, event | category | flops | bytes accessed | tf_op | source)
XLA Modules:
  0.0 87.5 jit_solution(7989006105115416898)
XLA Ops:
  0.6 84.7 %shard_map.67 = (bf16[256,3584]{1,0:T(8,128)(2,1)S(1)}, bf16[256,3584]{1,0:T(8,128)(2,1)S(1)}, bf16[3584,128]{1,0:T(8,128)(2,1)S(1)}) custom-call(bf16[128,2048]{1,0:T(8,128)(2,1)} %bitcast.9, bf16[256,3584]{1,0:T(8,128)(2,1)} %bitcast.5, bf16[256,3584]{1,0:T(8,128)(2,1)} %bitcast.6, bf16[3584,2048]{1,0:T(8,128)(2,1)} %w.1), custom_call_target="tpu_custom_call" | custom-call | flops 15032385536 | bytes 24000000 | tf_op jit(solution)/shard_map/pallas_call | solution.py:549
  85.3 2.2 %shard_map.68 = (bf16[256,3584]{1,0:T(8,128)(2,1)}, bf16[256,3584]{1,0:T(8,128)(2,1)}, bf16[3584,128]{1,0:T(8,128)(2,1)}) custom-call(bf16[256,3584]{1,0:T(8,128)(2,1)S(1)} %get-tuple-element.9.gate_v, bf16[256,3584]{1,0:T(8,128)(2,1)S(1)} %get-tuple-element.10.up_v, bf16[3584,128]{1,0:T(8,128)(2,1)S(1)} %get-tuple-element.11.weight_v), custom_call_target="tpu_custom_call" | custom-call | tf_op jit(solution)/shard_map/pallas_call | solution.py:560

commit v6 on v5

--- a/solution.py
+++ b/solution.py
@@ -75,7 +75,7 @@
 
     def own_direct(b, side):
         return send(
-            go.at[:, cols(b)], g_own.at[ds(x * ROWS, ROWS, ROWS), cols(b)],
+            g_own.at[ds(x * ROWS, ROWS, ROWS), cols(b)], g_own.at[ds(x * ROWS, ROWS, ROWS), cols(b)],
             xo_s.at[b, side], xo_r.at[b, side], sides[side],
         )
 
@@ -89,7 +89,7 @@
     def pair_send(j, s):
         i = j * 2 + s
         return send(
-            go.at[:, cols(block_of(j, s + 2))], g_pair.at[ds(x * ROWS, ROWS, ROWS), cols(i)],
+            g_own.at[ds(x * ROWS, ROWS, ROWS), cols(block_of(j, s + 2))], g_pair.at[ds(x * ROWS, ROWS, ROWS), cols(i)],
             pp_s.at[i], pp_r.at[i], pair,
         )
 
@@ -353,10 +353,11 @@
         for s in (0, 1):
             pair_send(j, s).start()
 
+    own_copy().start()
     loop(0, NC, load)
-    own_copy().start()
     w_copy(0).start()
     w_copy(1).start()
+    own_copy().wait()
     pl.semaphore_wait(barrier, 7)
     own_start(0, 0)
     pair_start(0)
@@ -367,7 +368,6 @@
     pair_start(2)
     pair_start(3)
     loop(1, 5, make_hidden)
-    own_copy().wait()
 
     def turn(j):
         own_end(j, 0)

time: 88.2 us -> 87.9 us (level)
  no operation moved by 1% of the time
where the time goes in v6:
time: 87.9 us; the launch traced here: 87.3 us
  Pallas kernels  86.7 us (99%)
    pallas_call x1, Pallas kernels, on_device(): pl.pallas_call(kernel, out_shape=(pltpu.VMEM((HALF, FF), BF16), pltpu.VME...  84.4 us
    pallas_call x1, Pallas kernels, on_device(): pl.pallas_call(write_out, out_shape=tuple((jax.ShapeDtypeStruct(r.shape,...  2.23 us

profile of v6, /device:TPU:1, one launch (start us, length us, event | category | flops | bytes accessed | tf_op | source)
XLA Modules:
  0.0 87.3 jit_solution(11593032936656340734)
XLA Ops:
  0.6 84.4 %shard_map.67 = (bf16[256,3584]{1,0:T(8,128)(2,1)S(1)}, bf16[256,3584]{1,0:T(8,128)(2,1)S(1)}, bf16[3584,128]{1,0:T(8,128)(2,1)S(1)}) custom-call(bf16[128,2048]{1,0:T(8,128)(2,1)} %bitcast.9, bf16[256,3584]{1,0:T(8,128)(2,1)} %bitcast.5, bf16[256,3584]{1,0:T(8,128)(2,1)} %bitcast.6, bf16[3584,2048]{1,0:T(8,128)(2,1)} %w.1), custom_call_target="tpu_custom_call" | custom-call | flops 15032385536 | bytes 24000000 | tf_op jit(solution)/shard_map/pallas_call | solution.py:549
  85.1 2.2 %shard_map.68 = (bf16[256,3584]{1,0:T(8,128)(2,1)}, bf16[256,3584]{1,0:T(8,128)(2,1)}, bf16[3584,128]{1,0:T(8,128)(2,1)}) custom-call(bf16[256,3584]{1,0:T(8,128)(2,1)S(1)} %get-tuple-element.9.gate_v, bf16[256,3584]{1,0:T(8,128)(2,1)S(1)} %get-tuple-element.10.up_v, bf16[3584,128]{1,0:T(8,128)(2,1)S(1)} %get-tuple-element.11.weight_v), custom_call_target="tpu_custom_call" | custom-call | tf_op jit(solution)/shard_map/pallas_call | solution.py:560
